TPU v7x, 32 devices: a whole 2x2x4 slice. The times are simulated.
32 devices in a mesh: seg: 8 (over z, x), tok: 4 (over y, core).
Axes of the slice: x: 2, y: 2, z: 4, core: 2. Of those that a mesh axis runs over, the one named last changes fastest.
Arguments:
- queries: bfloat16 [8192, 2048], P(('seg', 'tok')), may hold values from -40 to 40
- keys: bfloat16 [8192, 512], P(('seg', 'tok')), may hold values from -40 to 40
- values: bfloat16 [8192, 512], P(('seg', 'tok')), may hold values from -6 to 6
- gain_mem: float32 [2048], replicated, may hold values from 0.25 to 1.75
- gain_dot: float32 [2048], replicated, may hold values from 0.25 to 1.75
- out_weight: bfloat16 [2048, 2048], replicated, may hold values from -0.125 to 0.125
Outputs:
- layer_out: bfloat16 [8192, 2048], P(('seg', 'tok'))
All inputs are finite; a program needn't handle non-finite values.
Results may differ from a plain program's by a relative error of at most 0.008.
Values may be sent and summed in bfloat16 or wider, within the bound.
A program may use at most 128 MiB of HBM per device.

v0:
```python
import jax
import jax.numpy as jnp
from jax import lax
from jax.sharding import PartitionSpec as P

HEAD_DIMENSION = 128


def entering(shard, axis, join, neutral):
    place = lax.axis_index(axis)
    gathered = lax.all_gather(shard.astype(jnp.bfloat16), axis)
    state = jnp.zeros_like(shard) + jnp.asarray(neutral, shard.dtype)

    def one(lap, state):
        return join(state, lax.dynamic_index_in_dim(gathered, lap, 0, False).astype(shard.dtype))

    return lax.fori_loop(0, place, one, state)


def feature_map(inputs):
    return jax.nn.elu(inputs) + 1.0


def head_norm(inputs, gain):
    return inputs * lax.rsqrt(jnp.mean(inputs * inputs, axis=-1, keepdims=True) + 1e-06) * gain


def add_terms(earlier_terms, later_terms):
    return earlier_terms + later_terms


def local(queries, keys, values, gain_mem, gain_dot, out_weight):
    row_count = queries.shape[0]
    head_size = HEAD_DIMENSION
    heads_query = queries.shape[1] // head_size
    heads_value = keys.shape[1] // head_size
    query_group_width = heads_query // heads_value
    scale = float(head_size) ** (-0.5)
    first_row = lax.axis_index("tok") * row_count
    query_block = queries.reshape(row_count, heads_value, query_group_width, head_size)
    query_positions = first_row + jnp.arange(row_count, dtype=jnp.int32)
    sig_keys = (
        feature_map(keys.astype(jnp.float32))
        .astype(jnp.bfloat16)
        .reshape(row_count, heads_value, head_size)
    )
    value_heads_own = values.reshape(row_count, heads_value, head_size)
    partial_value = jnp.einsum(
        "rgd,rge->gde", sig_keys, value_heads_own, preferred_element_type=jnp.float32
    )
    owned = lax.psum_scatter(
        partial_value.astype(jnp.bfloat16), "tok", scatter_dimension=1, tiled=True
    ).astype(jnp.float32)
    earlier = entering(owned, "seg", add_terms, jnp.zeros_like(owned))
    earlier = lax.all_gather(earlier.astype(jnp.bfloat16), "tok", axis=1, tiled=True).astype(
        earlier.dtype
    )
    key_piece = lax.all_gather(keys, "tok", axis=0, tiled=True)
    value_piece = lax.all_gather(values, "tok", axis=0, tiled=True)
    piece_rows = key_piece.shape[0]
    key_heads = key_piece.reshape(piece_rows, heads_value, head_size)
    value_heads = value_piece.reshape(piece_rows, heads_value, head_size)
    key_positions = jnp.arange(piece_rows, dtype=jnp.int32)
    visible = query_positions[:, None] >= key_positions[None, :]
    scores = (
        jnp.einsum("rgjd,cgd->gjrc", query_block, key_heads, preferred_element_type=jnp.float32)
        * scale
    )
    scores = jnp.where(visible, scores, -1e30)
    running_max = jnp.full((heads_value, query_group_width, row_count, 1), -1e30, jnp.float32)
    new_max = jnp.maximum(running_max, jnp.max(scores, axis=-1, keepdims=True))
    weights = jnp.where(visible, jnp.exp(scores - new_max), 0.0)
    product = jnp.einsum(
        "gjrc,cgd->gjrd",
        weights.astype(jnp.bfloat16),
        value_heads,
        preferred_element_type=jnp.float32,
    )
    final_sum = jnp.sum(weights, axis=-1, keepdims=True)
    dot_part = jnp.transpose(product / final_sum, (2, 0, 1, 3)).reshape(
        row_count, heads_query, head_size
    )
    sig_queries = feature_map(query_block.astype(jnp.float32))
    memory_part = jnp.einsum(
        "rgjd,gde->rgje", sig_queries, earlier, precision=lax.Precision.HIGHEST
    )
    memory_part = memory_part.reshape(row_count, heads_query, head_size)
    gain_memory = gain_mem.reshape(heads_query, head_size)
    gain_attend = gain_dot.reshape(heads_query, head_size)
    mixed = (0.5 * (head_norm(memory_part, gain_memory) + head_norm(dot_part, gain_attend))).astype(
        jnp.bfloat16
    )
    mixed = mixed.reshape(row_count, heads_query * head_size)
    return jnp.dot(mixed, out_weight, preferred_element_type=jnp.float32).astype(jnp.bfloat16)


def solution(mesh):
    return jax.shard_map(
        local,
        mesh=mesh,
        in_specs=(
            P(("seg", "tok"), None),
            P(("seg", "tok"), None),
            P(("seg", "tok"), None),
            P(),
            P(),
            P(),
        ),
        out_specs=P(("seg", "tok"), None),
        check_vma=False,
    )
```

profile of v0, /device:TPU:0, one launch (start us, length us, event | category | flops | bytes accessed | tf_op | source)
XLA Modules:
  0.0 112.0 jit_solution(12363129356055053207)
XLA Ops:
  6.5 0.0 reduce-scatter.2.cloned.1.call-start
  6.5 1.2 %fusion.25 = bf16[256,512]{1,0:T(8,128)(2,1)S(1)} fusion(bf16[256,512]{1,0:T(8,128)(2,1)} %param.9), kind=kLoop, calls=%fused_computation.36 | loop fusion | flops 786432 | bytes 524288 | tf_op jit(solution)/shard_map/convert_element_type | solution.py:44
  7.7 0.1 copy.33
  7.9 1.8 %convolution_convert_fusion.1 = bf16[4,128,128]{2,1,0:T(8,128)(2,1)} fusion(bf16[256,4,128]{0,2,1:T(8,128)(2,1)S(1)} %bitcast.85, bf16[256,512]{1,0:T(8,128)(2,1)} %param.10), kind=kOutput, calls=%fused_computation.27 | convolution fusion | flops 33619968 | bytes 655360 | tf_op jit(solution)/shard_map/rgd,rge->gde/dot_general | solution.py:48
  9.7 0.0 reduce-scatter.2.cloned.1.call-update
  9.7 0.0 all-gather.4.cloned.1.call-start
  9.7 1.8 %copy.24 = bf16[256,512]{0,1:T(8,128)(2,1)} copy(bf16[256,512]{1,0:T(8,128)(2,1)} %param.9) | data formatting | bytes 524288 | tf_op args[1]
  11.5 0.0 all-gather.4.cloned.1.call-update
  11.6 0.0 all-gather.6.cloned.1.call-start
  11.6 0.7 all-gather.6.cloned.1.call-update
  12.3 0.2 iota_compare_fusion
  12.5 1.8 %reshape.79 = bf16[256,4,4,128]{3,2,1,0:T(4,128)(2,1)S(1)} reshape(bf16[256,2048]{1,0:T(8,128)(2,1)} %param.8) | data formatting | bytes 2097152 | tf_op jit(solution)/shard_map/reshape | solution.py:40
  14.3 17.8 %reduce-scatter.2.cloned.1.call-done = bf16[4,32,128]{2,1,0:T(8,128)(2,1)} async-done(((bf16[4,128,128]{2,1,0:T(8,128)(2,1)}), bf16[4,32,128]{2,1,0:T(8,128)(2,1)}) %reduce-scatter.2.cloned.1.call-update) | async-done | bytes 32784 | tf_op jit(solution)/shard_map/reduce_scatter | solution.py:51
  32.1 31.0 %all-gather = bf16[32,32,128]{2,1,0:T(8,128)(2,1)S(1)} all-gather(bf16[4,32,128]{2,1,0:T(8,128)(2,1)} %reduce-scatter.2.cloned.1.call-done), channel_id=2, replica_groups=mesh['seg'=8,'tok'=4] {'seg'}, dimensions={0}, use_global_device_ids=true | all-gather | bytes 294912 | tf_op jit(solution)/shard_map/all_gather | solution.py:11
  63.2 5.9 %all_gather.17 = bf16[4,128,128]{2,1,0:T(8,128)(2,1)S(1)} all-gather(bf16[4,32,128]{2,1,0:T(8,128)(2,1)S(1)} %convert_element_type.37), channel_id=1, replica_groups=mesh['seg'=8,'tok'=4] {'tok'}, dimensions={1}, use_global_device_ids=true | all-gather | bytes 163840 | tf_op jit(solution)/shard_map/all_gather | solution.py:55
  69.1 2.2 %fusion.15 = (f32[256,4,4]{0,2,1:T(4,128)S(1)}, f32[4,128,256,4]{2,1,3,0:T(8,128)S(1)}) fusion(bf16[256,4,4,128]{3,2,1,0:T(4,128)(2,1)S(1)} %reshape.79, bf16[4,128,128]{2,1,0:T(8,128)(2,1)S(1)} %all_gather.17), kind=kOutput, calls=%fused_computation.23 | convolution fusion | flops 808972288 | bytes 3293184 | tf_op jit(solution)/shard_map/rgjd,gde->rgje/dot_general | solution.py:84
  71.3 0.0 all-gather.4.cloned.1.call-done
  71.3 4.3 %fusion = (f32[4,4,256]{2,1,0:T(4,128)S(1)}, f32[4,1024,256,4]{2,1,3,0:T(8,128)S(1)}) fusion(pred[256,1024]{0,1:T(8,128)(4,1)S(1)} %iota_compare_fusion, bf16[1024,4,128,1]{0,2,3,1:T(8,128)(2,1)} %bitcast.83, bf16[256,4,4,128]{3,2,1,0:T(4,128)(2,1)S(1)} %reshape.79), kind=kOutput, calls=%fused_computation.3 | convolution fusion | flops 1086320640 | bytes 19152896 | tf_op jit(solution)/shard_map/rgjd,cgd->gjrc/dot_general | solution.py:66
  75.7 0.0 copy-start
  75.7 5.7 %copy-done = f32[4,1024,256,4]{2,1,3,0:T(8,128)} copy-done((f32[4,1024,256,4]{2,1,3,0:T(8,128)}, f32[4,1024,256,4]{2,1,3,0:T(8,128)S(1)}, u32[]{:S(2)}) %copy-start) | copy-done | bytes 16777240
  81.4 4.0 %fusion.1 = f32[4,4,256]{2,1,0:T(4,128)S(1)} fusion(f32[4,1024,256,4]{2,1,3,0:T(8,128)S(1)} %get-tuple-element.38, f32[4,4,256]{2,1,0:T(4,128)S(1)} %broadcast_maximum_fusion, pred[256,1024]{0,1:T(8,128)(4,1)S(1)} %iota_compare_fusion), kind=kLoop, calls=%fused_computation.4 | loop fusion | flops 20967424 | bytes 17072128 | tf_op jit(solution)/shard_map/reduce_sum | solution.py:79
  85.4 0.0 all-gather.6.cloned.1.call-done
  85.5 1.5 %copy.27 = bf16[1024,512]{0,1:T(8,128)(2,1)S(1)} copy(bf16[1024,512]{1,0:T(8,128)(2,1)} %all-gather.6.cloned.1.call-done) | data formatting | bytes 2097152 | tf_op jit(solution)/shard_map/all_gather | solution.py:59
  86.9 0.0 copy-start.1
  87.0 0.0 copy-start.2
  87.0 9.7 %multiply_reduce_fusion = (f32[256,4,4]{0,2,1:T(4,128)S(1)}, f32[256,4,4,128]{0,3,2,1:T(8,128)}) fusion(f32[256,4,4]{0,2,1:T(4,128)S(1)} %bitcast.87, bf16[1024,4,128,1]{0,2,3,1:T(8,128)(2,1)S(1)} %bitcast.84, f32[4,1024,256,4]{2,1,3,0:T(8,128)} %copy-done, f32[4,4,256]{2,1,0:T(4,128)S(1)} %broadcast_maximum_fusion, pred[256,1024]{0,1:T(8,128)(4,1)S(1)} %iota_compare_fusion), kind=kOutput, calls=%fused_computation.24 | convolution fusion | flops 1096282112 | bytes 20234240 | tf_op jit(solution)/shard_map/gjrc,cgd->gjrd/dot_general | solution.py:73
  96.7 0.0 copy-done.1
  96.7 0.0 copy-done.2
  96.7 2.0 %fusion.13 = bf16[256,2048]{0,1:T(8,128)(2,1)S(1)} fusion(f32[4,128,256,4]{2,1,3,0:T(8,128)S(1)} %get-tuple-element.42, f32[256,4,4,128]{0,3,2,1:T(8,128)} %get-tuple-element.40, f32[2048]{0:T(1024)S(1)} %copy-done.1, f32[256,16]{0,1:T(8,128)S(1)} %rsqrt.25, f32[2048]{0:T(1024)S(1)} %copy-done.2, f32[256,16]{0,1:T(8,128)S(1)} %rsqrt.23), kind=kLoop, calls=%fused_computation.18 | loop fusion | flops 3670016 | bytes 5292032 | tf_op jit(solution)/shard_map/convert_element_type | solution.py:90
  98.7 6.7 %convolution_convert_fusion = bf16[256,2048]{1,0:T(8,128)(2,1)} fusion(bf16[256,2048]{0,1:T(8,128)(2,1)S(1)} %fusion.13, bf16[2048,2048]{1,0:T(8,128)(2,1)} %param.13), kind=kOutput, calls=%fused_computation.10 | convolution fusion | flops 2148007936 | bytes 10485760 | tf_op jit(solution)/shard_map/dot_general | solution.py:94
  (9 shorter events, 0.1 us)
Async XLA Ops:
  6.5 25.6 %reduce-scatter.2.cloned.1.call-start = ((), (), s32[]{:S(2)}) async-start(), calls=%async_computation.1 | async-start | bytes 163840 | tf_op jit(solution)/shard_map/reduce_scatter | solution.py:51
  9.7 61.6 %all-gather.4.cloned.1.call-start = ((), (), s32[]{:S(2)}) async-start(), calls=%async_computation.2 | async-start | bytes 1310720 | tf_op jit(solution)/shard_map/all_gather | solution.py:58
  11.6 73.9 %all-gather.6.cloned.1.call-start = ((), (), s32[]{:S(2)}) async-start(), calls=%async_computation.3 | async-start | bytes 1310720 | tf_op jit(solution)/shard_map/all_gather | solution.py:59
  75.7 5.7 %copy-start = (f32[4,1024,256,4]{2,1,3,0:T(8,128)}, f32[4,1024,256,4]{2,1,3,0:T(8,128)S(1)}, u32[]{:S(2)}) copy-start(f32[4,1024,256,4]{2,1,3,0:T(8,128)S(1)} %get-tuple-element.38) | copy-start | bytes 50331652
  86.9 9.7 %copy-start.1 = (f32[2048]{0:T(1024)S(1)}, f32[2048]{0:T(1024)}, u32[]{:S(2)}) copy-start(f32[2048]{0:T(1024)} %param.12) | copy-start | bytes 24580
  87.0 9.7 %copy-start.2 = (f32[2048]{0:T(1024)S(1)}, f32[2048]{0:T(1024)}, u32[]{:S(2)}) copy-start(f32[2048]{0:T(1024)} %param.11) | copy-start | bytes 24580
Sparse Core Ops, SparseCore 0:
  9.8 22.2 reduce-scatter.1
  33.8 16.8 all-gather.3
  52.3 17.4 all-gather.5
where the time goes:
time: 112 us
  blocking collectives  36.9 us (33%)
  matrix products  24.7 us (22%)
  waiting for transfers between devices  18.6 us (17%)
  between operations  13.3 us (12%)
  local copies, waits for them, and re-layouts  10.9 us (10%)
  other arithmetic  7.45 us (7%)
    all_gather x1, blocking collectives, entering(): gathered = lax.all_gather(shard.astype(jnp.bfloat16), axis)  31 us
    reduce_scatter x1, waiting for transfers between devices, local(): lax.psum_scatter(partial_value.astype(jnp.bfloat16), 'tok', scatter_dimen...  17.8 us
    dot_general x1, matrix products, local(): jnp.einsum('gjrc,cgd->gjrd', weights.astype(jnp.bfloat16), value_heads, p...  9.65 us
    unnamed x7, local copies, waits for them, and re-layouts  7.5 us
    dot_general x1, matrix products, local(): jnp.dot(mixed, out_weight, preferred_element_type=jnp.float32)  6.72 us
    all_gather x1, blocking collectives, local(): lax.all_gather(earlier.astype(jnp.bfloat16), 'tok', axis=1, tiled=True)  5.9 us
    dot_general x1, matrix products, local(): jnp.einsum('rgjd,cgd->gjrc', query_block, key_heads, preferred_element_ty...  4.33 us
    reduce_sum x1, other arithmetic, local(): final_sum = jnp.sum(weights, axis=-1, keepdims=True)  4.03 us
  transfers between devices with their start and end apart: 3, of which 1 were waited for; matrix products, arithmetic and copies ran while one was open for 13% of the time, Pallas kernels for 0%

commit v1 on v0

v1 whole, which is shorter than its diff:
```python
import functools

import jax
import jax.numpy as jnp
from jax import lax
from jax.experimental import pallas as pl
from jax.experimental.pallas import tpu as pltpu
from jax.sharding import PartitionSpec as P

HEAD = 128
MESH = pl.DeviceIdType.MESH
LOG2E = 1.4426950408889634


def feature_map(x):
    return jnp.where(x > 0.0, x + 1.0, jnp.exp(x))


def norm(x, gain):
    return x * lax.rsqrt(jnp.mean(x * x, axis=-1, keepdims=True) + 1e-06) * gain


def kernel(
    n_seg, n_tok, groups, per_group,
    q_ref, k_ref, v_ref, gain_mem_ref, gain_dot_ref, mixed_ref,
    kv, parts, terms, own, earlier, memory, dots,
    kv_recv, far_send, mate_send, part_send, part_recv,
    own_send, earlier_recv, memory_send, memory_recv,
):
    seg = lax.axis_index("seg")
    tok = lax.axis_index("tok")
    rows = q_ref.shape[0]
    share = HEAD // n_tok
    cores = 2 if n_tok % 2 == 0 else 1
    chips = n_tok // cores
    core = lax.rem(tok, cores)
    mate = tok + 1 - 2 * core if cores == 2 else tok

    barrier = pltpu.get_barrier_semaphore()
    for step in range(1, n_tok):
        pl.semaphore_signal(
            barrier, inc=1, device_id={"tok": lax.rem(tok + step, n_tok)}, device_id_type=MESH
        )

    def greet(step, carry):
        pl.semaphore_signal(
            barrier, inc=1, device_id={"seg": lax.rem(seg + step, n_seg)}, device_id_type=MESH
        )
        return carry

    lax.fori_loop(1, n_seg, greet, 0)

    for g in range(groups):
        columns = slice(g * HEAD, (g + 1) * HEAD)
        key, value = k_ref[:, columns], v_ref[:, columns]
        kv[tok, g, 0] = key
        kv[tok, g, 1] = value
        sig = feature_map(key.astype(jnp.float32)).astype(jnp.bfloat16)
        part = lax.dot_general(
            sig, value, (((0,), (0,)), ((), ())), preferred_element_type=jnp.float32
        )
        parts[:, g] = part.astype(jnp.bfloat16).reshape(n_tok, share, HEAD)
    pl.semaphore_wait(barrier, n_tok - 1 + n_seg - 1)

    def remote(src, dst, send, recv, device):
        return pltpu.make_async_remote_copy(
            src_ref=src, dst_ref=dst, send_sem=send, recv_sem=recv,
            device_id=device, device_id_type=MESH,
        )

    def part_copy(step):
        peer = lax.rem(tok + step, n_tok)
        return remote(
            parts.at[peer], terms.at[tok], part_send.at[step], part_recv.at[step], {"tok": peer}
        )

    def part_arrival(step):
        source = lax.rem(tok + n_tok - step, n_tok)
        return remote(
            parts.at[source], terms.at[source], part_send.at[step], part_recv.at[step],
            {"tok": source},
        )

    def own_copy(peer):
        return remote(
            own, earlier.at[seg], own_send.at[peer], earlier_recv.at[seg], {"seg": peer}
        )

    def own_arrival(source):
        return remote(
            own, earlier.at[source], own_send.at[source], earlier_recv.at[source],
            {"seg": source},
        )

    def memory_copy(step):
        peer = lax.rem(tok + step, n_tok)
        return remote(
            memory.at[tok], memory.at[tok], memory_send.at[step], memory_recv.at[step],
            {"tok": peer},
        )

    def memory_arrival(step):
        source = lax.rem(tok + n_tok - step, n_tok)
        return remote(
            memory.at[source], memory.at[source], memory_send.at[step], memory_recv.at[step],
            {"tok": source},
        )

    def far_copy(hop, g):
        return remote(
            kv.at[tok, g], kv.at[tok, g], far_send.at[hop, g], kv_recv.at[tok, g],
            {"tok": tok + cores * hop},
        )

    def mate_copy(block, g):
        return remote(
            kv.at[block, g], kv.at[block, g], mate_send.at[block, g], kv_recv.at[block, g],
            {"tok": mate},
        )

    for step in range(1, n_tok):
        part_copy(step).start()

    def send_keys(g, carry):
        for hop in range(1, chips):
            @pl.when(tok + cores * hop < n_tok)
            def _():
                far_copy(hop, g).start()

        if cores == 2:
            @pl.when(core == 0)
            def _():
                mate_copy(tok, g).start()
        return carry

    lax.fori_loop(0, groups, send_keys, 0)

    terms[tok] = parts[tok]
    for step in range(1, n_tok):
        part_arrival(step).wait_recv()
    total = terms[0].astype(jnp.float32)
    for j in range(1, n_tok):
        total += terms[j].astype(jnp.float32)
    own[...] = total.astype(jnp.bfloat16)

    def send_own(peer, carry):
        own_copy(peer).start()
        return carry

    lax.fori_loop(seg + 1, n_seg, send_own, 0)

    def gather_earlier():
        def add(source, state):
            own_arrival(source).wait_recv()
            return state + earlier[source].astype(jnp.float32)

        state = lax.fori_loop(0, seg, add, jnp.zeros((groups, share, HEAD), jnp.float32))
        memory[tok] = state.astype(jnp.bfloat16)
        for step in range(1, n_tok):
            memory_copy(step).start()

    def forward(t, g):
        for block in range(t - cores, -1, -cores):
            mate_copy(block, g).wait_recv()
            if cores == 2:
                mate_copy(block, g).start()

    def attend(t, g):
        if cores == 2:
            for block in range(t):
                if block % 2 != t % 2:
                    mate_copy(block, g).wait_recv()
        row = lax.broadcasted_iota(jnp.int32, (rows, rows), 0)
        column = lax.broadcasted_iota(jnp.int32, (rows, rows), 1)
        ones = jnp.ones((rows, HEAD), jnp.bfloat16)
        for j in range(per_group):
            if j == per_group // 2:
                @pl.when(g + 1 < groups)
                def _():
                    forward(t, g + 1)
            columns = pl.ds(pl.multiple_of((g * per_group + j) * HEAD, HEAD), HEAD)
            query = q_ref[:, columns]
            scores = [
                lax.dot_general(
                    query, kv[b, g, 0], (((1,), (1,)), ((), ())),
                    preferred_element_type=jnp.float32,
                )
                for b in range(t + 1)
            ]
            scores[t] = jnp.where(row >= column, scores[t], -1e30)
            top = functools.reduce(jnp.maximum, scores)
            top = jnp.max(top, axis=-1, keepdims=True)
            acc = None
            for b in range(t + 1):
                weights = jnp.exp2((scores[b] - top) * (HEAD ** -0.5 * LOG2E))
                term = jnp.dot(
                    weights.astype(jnp.bfloat16),
                    jnp.concatenate([kv[b, g, 1], ones], axis=1),
                    preferred_element_type=jnp.float32,
                )
                acc = term if acc is None else acc + term
            read = acc[:, :HEAD] / acc[:, HEAD:]
            dots[:, columns] = norm(read, gain_dot_ref[:, columns])

    for t in range(n_tok):
        @pl.when(tok == t)
        def _():
            forward(t, 0)

    def group(g, carry):
        for t in range(n_tok):
            @pl.when(tok == t)
            def _():
                attend(t, g)

        @pl.when(g == 0)
        def _():
            gather_earlier()
        return carry

    lax.fori_loop(0, groups, group, 0)

    for step in range(1, n_tok):
        memory_arrival(step).wait_recv()

    def mix(g, carry):
        rows_memory = memory[:, g].reshape(HEAD, HEAD)
        for j in range(per_group):
            columns = pl.ds(pl.multiple_of((g * per_group + j) * HEAD, HEAD), HEAD)
            sig = feature_map(q_ref[:, columns].astype(jnp.float32)).astype(jnp.bfloat16)
            read = jnp.dot(sig, rows_memory, preferred_element_type=jnp.float32)
            read = norm(read, gain_mem_ref[:, columns])
            mixed_ref[:, columns] = (0.5 * (read + dots[:, columns])).astype(jnp.bfloat16)
        return carry

    lax.fori_loop(0, groups, mix, 0)

    for step in range(1, n_tok):
        part_copy(step).wait_send()
        memory_copy(step).wait_send()

    def sent_own(peer, carry):
        own_copy(peer).wait_send()
        return carry

    lax.fori_loop(seg + 1, n_seg, sent_own, 0)

    def sent_keys(g, carry):
        for hop in range(1, chips):
            @pl.when(tok + cores * hop < n_tok)
            def _():
                far_copy(hop, g).wait_send()

            if cores == 2:
                @pl.when(tok >= cores * hop)
                def _():
                    mate_copy(tok - cores * hop, g).wait_send()

        if cores == 2:
            @pl.when(core == 0)
            def _():
                mate_copy(tok, g).wait_send()
        return carry

    lax.fori_loop(0, groups, sent_keys, 0)


def local(n_seg, n_tok, queries, keys, values, gain_mem, gain_dot, out_weight):
    rows, width = queries.shape
    groups = keys.shape[1] // HEAD
    per_group = width // HEAD // groups
    share = HEAD // n_tok
    vmem = pl.BlockSpec(memory_space=pltpu.VMEM)
    dma = pltpu.SemaphoreType.DMA
    mixed = pl.pallas_call(
        functools.partial(kernel, n_seg, n_tok, groups, per_group),
        out_shape=jax.ShapeDtypeStruct((rows, width), jnp.bfloat16),
        in_specs=[vmem] * 5,
        out_specs=vmem,
        scratch_shapes=[
            pltpu.VMEM((n_tok, groups, 2, rows, HEAD), jnp.bfloat16),
            pltpu.VMEM((n_tok, groups, share, HEAD), jnp.bfloat16),
            pltpu.VMEM((n_tok, groups, share, HEAD), jnp.bfloat16),
            pltpu.VMEM((groups, share, HEAD), jnp.bfloat16),
            pltpu.VMEM((n_seg, groups, share, HEAD), jnp.bfloat16),
            pltpu.VMEM((n_tok, groups, share, HEAD), jnp.bfloat16),
            pltpu.VMEM((rows, width), jnp.float32),
            dma((n_tok, groups)),
            dma((n_tok, groups)),
            dma((n_tok, groups)),
            dma((n_tok,)),
            dma((n_tok,)),
            dma((n_seg,)),
            dma((n_seg,)),
            dma((n_tok,)),
            dma((n_tok,)),
        ],
        compiler_params=pltpu.CompilerParams(
            collective_id=0, has_side_effects=True, vmem_limit_bytes=32 * 1024 * 1024
        ),
    )(queries, keys, values, gain_mem.reshape(1, width), gain_dot.reshape(1, width))
    return jnp.dot(mixed, out_weight, preferred_element_type=jnp.float32).astype(jnp.bfloat16)


def solution(mesh):
    return jax.shard_map(
        functools.partial(local, mesh.shape["seg"], mesh.shape["tok"]),
        mesh=mesh,
        in_specs=(
            P(("seg", "tok"), None),
            P(("seg", "tok"), None),
            P(("seg", "tok"), None),
            P(),
            P(),
            P(),
        ),
        out_specs=P(("seg", "tok"), None),
        check_vma=False,
    )
```

time: 112 us -> 36.7 us (0.33)
  the two profiles are of different devices: /device:TPU:0 before, /device:TPU:5 now
where the time goes in v1:
time: 36.7 us; the launch traced here: 36.4 us
  Pallas kernels  25.2 us (69%)
  matrix products  6.68 us (18%)
  local copies, waits for them, and re-layouts  4.52 us (12%)
    pallas_call x1, Pallas kernels, local(): pl.pallas_call(functools.partial(kernel, n_seg, n_tok, groups, per_group)...  25.2 us
    dot_general x1, matrix products, local(): jnp.dot(mixed, out_weight, preferred_element_type=jnp.float32)  6.68 us
    unnamed x10, local copies, waits for them, and re-layouts  4.52 us

profile of v1, /device:TPU:5, one launch (start us, length us, event | category | flops | bytes accessed | tf_op | source)
XLA Modules:
  0.0 36.4 jit_solution(1197539677410583965)
XLA Ops:
  0.0 0.0 copy-start
  0.0 1.2 %copy-done = bf16[256,2048]{1,0:T(8,128)(2,1)S(1)} copy-done((bf16[256,2048]{1,0:T(8,128)(2,1)S(1)}, bf16[256,2048]{1,0:T(8,128)(2,1)}, u32[]{:S(2)}) %copy-start) | copy-done | bytes 1048600
  1.2 0.0 copy-start.1
  1.2 0.9 %copy-done.1 = bf16[256,512]{1,0:T(8,128)(2,1)S(1)} copy-done((bf16[256,512]{1,0:T(8,128)(2,1)S(1)}, bf16[256,512]{1,0:T(8,128)(2,1)}, u32[]{:S(2)}) %copy-start.1) | copy-done | bytes 262168
  2.2 0.0 copy-start.2
  2.2 0.9 %copy-done.2 = bf16[256,512]{1,0:T(8,128)(2,1)S(1)} copy-done((bf16[256,512]{1,0:T(8,128)(2,1)S(1)}, bf16[256,512]{1,0:T(8,128)(2,1)}, u32[]{:S(2)}) %copy-start.2) | copy-done | bytes 262168
  3.1 0.0 copy-start.3
  3.1 0.7 %copy-done.3 = f32[2048]{0:T(1024)S(1)} copy-done((f32[2048]{0:T(1024)S(1)}, f32[2048]{0:T(1024)}, u32[]{:S(2)}) %copy-start.3) | copy-done | bytes 8216
  3.8 0.0 copy-start.4
  3.8 0.7 %copy-done.4 = f32[2048]{0:T(1024)S(1)} copy-done((f32[2048]{0:T(1024)S(1)}, f32[2048]{0:T(1024)}, u32[]{:S(2)}) %copy-start.4) | copy-done | bytes 8216
  4.5 25.2 %shard_map.64 = bf16[256,2048]{1,0:T(8,128)(2,1)S(1)} custom-call(bf16[256,2048]{1,0:T(8,128)(2,1)S(1)} %copy-done, bf16[256,512]{1,0:T(8,128)(2,1)S(1)} %copy-done.1, bf16[256,512]{1,0:T(8,128)(2,1)S(1)} %copy-done.2, f32[1,2048]{1,0:T(1,128)S(1)} %bitcast.4, f32[1,2048]{1,0:T(1,128)S(1)} %bitcast.5), custom_call_target="tpu_custom_call" | custom-call | tf_op jit(solution)/shard_map/pallas_call | solution.py:275
  29.7 6.7 %convolution_convert_fusion = bf16[256,2048]{1,0:T(8,128)(2,1)} fusion(bf16[256,2048]{1,0:T(8,128)(2,1)S(1)} %shard_map.64, bf16[2048,2048]{1,0:T(8,128)(2,1)} %param.11), kind=kOutput, calls=%fused_computation | convolution fusion | flops 2148007936 | bytes 10485760 | tf_op jit(solution)/shard_map/dot_general | solution.py:302
Async XLA Ops:
  0.0 1.2 %copy-start = (bf16[256,2048]{1,0:T(8,128)(2,1)S(1)}, bf16[256,2048]{1,0:T(8,128)(2,1)}, u32[]{:S(2)}) copy-start(bf16[256,2048]{1,0:T(8,128)(2,1)} %q_ref.1) | copy-start | bytes 3145732
  1.2 0.9 %copy-start.1 = (bf16[256,512]{1,0:T(8,128)(2,1)S(1)}, bf16[256,512]{1,0:T(8,128)(2,1)}, u32[]{:S(2)}) copy-start(bf16[256,512]{1,0:T(8,128)(2,1)} %k_ref.1) | copy-start | bytes 786436
  2.2 0.9 %copy-start.2 = (bf16[256,512]{1,0:T(8,128)(2,1)S(1)}, bf16[256,512]{1,0:T(8,128)(2,1)}, u32[]{:S(2)}) copy-start(bf16[256,512]{1,0:T(8,128)(2,1)} %v_ref.1) | copy-start | bytes 786436
  3.1 0.7 %copy-start.3 = (f32[2048]{0:T(1024)S(1)}, f32[2048]{0:T(1024)}, u32[]{:S(2)}) copy-start(f32[2048]{0:T(1024)} %param.9) | copy-start | bytes 24580
  3.8 0.7 %copy-start.4 = (f32[2048]{0:T(1024)S(1)}, f32[2048]{0:T(1024)}, u32[]{:S(2)}) copy-start(f32[2048]{0:T(1024)} %param.10) | copy-start | bytes 24580

commit v2 on v1

--- a/solution.py
+++ b/solution.py
@@ -22,20 +22,32 @@
 
 def kernel(
     n_seg, n_tok, groups, per_group,
-    q_ref, k_ref, v_ref, gain_mem_ref, gain_dot_ref, mixed_ref,
+    q_hbm, k_hbm, v_hbm, gain_mem_hbm, gain_dot_hbm, weight_hbm, out_ref,
+    q_ref, k_ref, v_ref, gain_mem_ref, gain_dot_ref, weight_ref, mixed_ref,
     kv, parts, terms, own, earlier, memory, dots,
-    kv_recv, far_send, mate_send, part_send, part_recv,
+    load, kv_recv, far_send, mate_send, part_send, part_recv,
     own_send, earlier_recv, memory_send, memory_recv,
 ):
     seg = lax.axis_index("seg")
     tok = lax.axis_index("tok")
-    rows = q_ref.shape[0]
+    rows = q_hbm.shape[0]
     share = HEAD // n_tok
     cores = 2 if n_tok % 2 == 0 else 1
     chips = n_tok // cores
     core = lax.rem(tok, cores)
     mate = tok + 1 - 2 * core if cores == 2 else tok
 
+    loads = [
+        pltpu.make_async_copy(src, dst, load.at[i])
+        for i, (src, dst) in enumerate((
+            (k_hbm, k_ref), (v_hbm, v_ref), (q_hbm, q_ref),
+            (gain_mem_hbm, gain_mem_ref), (gain_dot_hbm, gain_dot_ref),
+            (weight_hbm, weight_ref),
+        ))
+    ]
+    for copy in loads:
+        copy.start()
+
     barrier = pltpu.get_barrier_semaphore()
     for step in range(1, n_tok):
         pl.semaphore_signal(
@@ -50,6 +62,8 @@
 
     lax.fori_loop(1, n_seg, greet, 0)
 
+    for copy in loads[:2]:
+        copy.wait()
     for g in range(groups):
         columns = slice(g * HEAD, (g + 1) * HEAD)
         key, value = k_ref[:, columns], v_ref[:, columns]
@@ -148,6 +162,8 @@
         return carry
 
     lax.fori_loop(seg + 1, n_seg, send_own, 0)
+    for copy in loads[2:5]:
+        copy.wait()
 
     def gather_earlier():
         def add(source, state):
@@ -234,6 +250,17 @@
         return carry
 
     lax.fori_loop(0, groups, mix, 0)
+    loads[5].wait()
+    tile = min(256, out_ref.shape[1])
+
+    def project(n, carry):
+        columns = pl.ds(pl.multiple_of(n * tile, tile), tile)
+        out_ref[:, columns] = jnp.dot(
+            mixed_ref[...], weight_ref[:, columns], preferred_element_type=jnp.float32
+        ).astype(jnp.bfloat16)
+        return carry
+
+    lax.fori_loop(0, out_ref.shape[1] // tile, project, 0)
 
     for step in range(1, n_tok):
         part_copy(step).wait_send()
@@ -272,12 +299,20 @@
     share = HEAD // n_tok
     vmem = pl.BlockSpec(memory_space=pltpu.VMEM)
     dma = pltpu.SemaphoreType.DMA
-    mixed = pl.pallas_call(
+    hbm = pl.BlockSpec(memory_space=pltpu.HBM)
+    return pl.pallas_call(
         functools.partial(kernel, n_seg, n_tok, groups, per_group),
-        out_shape=jax.ShapeDtypeStruct((rows, width), jnp.bfloat16),
-        in_specs=[vmem] * 5,
+        out_shape=jax.ShapeDtypeStruct((rows, out_weight.shape[1]), jnp.bfloat16),
+        in_specs=[hbm] * 6,
         out_specs=vmem,
         scratch_shapes=[
+            pltpu.VMEM(queries.shape, jnp.bfloat16),
+            pltpu.VMEM(keys.shape, jnp.bfloat16),
+            pltpu.VMEM(values.shape, jnp.bfloat16),
+            pltpu.VMEM((1, width), jnp.float32),
+            pltpu.VMEM((1, width), jnp.float32),
+            pltpu.VMEM(out_weight.shape, jnp.bfloat16),
+            pltpu.VMEM((rows, width), jnp.bfloat16),
             pltpu.VMEM((n_tok, groups, 2, rows, HEAD), jnp.bfloat16),
             pltpu.VMEM((n_tok, groups, share, HEAD), jnp.bfloat16),
             pltpu.VMEM((n_tok, groups, share, HEAD), jnp.bfloat16),
@@ -285,6 +320,7 @@
             pltpu.VMEM((n_seg, groups, share, HEAD), jnp.bfloat16),
             pltpu.VMEM((n_tok, groups, share, HEAD), jnp.bfloat16),
             pltpu.VMEM((rows, width), jnp.float32),
+            dma((6,)),
             dma((n_tok, groups)),
             dma((n_tok, groups)),
             dma((n_tok, groups)),
@@ -296,10 +332,9 @@
             dma((n_tok,)),
         ],
         compiler_params=pltpu.CompilerParams(
-            collective_id=0, has_side_effects=True, vmem_limit_bytes=32 * 1024 * 1024
+            collective_id=0, has_side_effects=True, vmem_limit_bytes=62 * 1024 * 1024
         ),
-    )(queries, keys, values, gain_mem.reshape(1, width), gain_dot.reshape(1, width))
-    return jnp.dot(mixed, out_weight, preferred_element_type=jnp.float32).astype(jnp.bfloat16)
+    )(queries, keys, values, gain_mem.reshape(1, width), gain_dot.reshape(1, width), out_weight)
 
 
 def solution(mesh):

time: 36.7 us -> 32.4 us (0.88)
  matrix products: 6.68 us -> 0 us
  Pallas kernels: 25.2 us -> 30 us
  local copies, waits for them, and re-layouts: 4.52 us -> 2.3 us
    dot_general x1 -> x0, matrix products: 6.68 us -> none  [local(): jnp.dot(mixed, out_weight, preferred_element_type=jnp.float32)]
    pallas_call x1, Pallas kernels: 25.2 us -> 30 us  [local(): pl.pallas_call(functools.partial(kernel, n_seg, n_tok, groups, per_group)...]
    unnamed x10 -> x1, local copies, waits for them, and re-layouts: 4.52 us -> 2.3 us
where the time goes in v2:
time: 32.4 us; the launch traced here: 32.3 us
  Pallas kernels  30 us (93%)
  local copies, waits for them, and re-layouts  2.3 us (7%)
    pallas_call x1, Pallas kernels, local(): pl.pallas_call(functools.partial(kernel, n_seg, n_tok, groups, per_group)...  30 us
    unnamed x1, local copies, waits for them, and re-layouts  2.3 us

profile of v2, /device:TPU:5, one launch (start us, length us, event | category | flops | bytes accessed | tf_op | source)
XLA Modules:
  0.0 32.3 jit_solution(12762188583500717343)
XLA Ops:
  0.0 30.0 %shard_map.64 = bf16[256,2048]{1,0:T(8,128)(2,1)} custom-call(bf16[256,2048]{1,0:T(8,128)(2,1)} %q_hbm.1, bf16[256,512]{1,0:T(8,128)(2,1)} %k_hbm.1, bf16[256,512]{1,0:T(8,128)(2,1)} %v_hbm.1, f32[1,2048]{1,0:T(1,128)} %bitcast.2, f32[1,2048]{1,0:T(1,128)} %bitcast.3, bf16[2048,2048]{1,0:T(8,128)(2,1)} %weight_hbm.1), custom_call_target="tpu_custom_call" | custom-call | tf_op jit(solution)/shard_map/pallas_call | solution.py:303
  30.0 2.3 %copy.8 = bf16[256,2048]{1,0:T(8,128)(2,1)} copy(bf16[256,2048]{1,0:T(8,128)(2,1)} %shard_map.64) | data formatting | bytes 2097152

commit v3 on v2

--- a/solution.py
+++ b/solution.py
@@ -249,9 +249,9 @@
             mixed_ref[:, columns] = (0.5 * (read + dots[:, columns])).astype(jnp.bfloat16)
         return carry
 
-    lax.fori_loop(0, groups, mix, 0)
+    lax.fori_loop(0, groups, mix, 0, unroll=True)
     loads[5].wait()
-    tile = min(256, out_ref.shape[1])
+    tile = min(512, out_ref.shape[1])
 
     def project(n, carry):
         columns = pl.ds(pl.multiple_of(n * tile, tile), tile)

time: 32.4 us -> 31.1 us (0.960)
  Pallas kernels: 30 us -> 28.6 us
    pallas_call x1, Pallas kernels: 30 us -> 28.6 us  [local(): pl.pallas_call(functools.partial(kernel, n_seg, n_tok, groups, per_group)...]
where the time goes in v3:
time: 31.1 us; the launch traced here: 30.9 us
  Pallas kernels  28.6 us (92%)
  local copies, waits for them, and re-layouts  2.3 us (7%)
    pallas_call x1, Pallas kernels, local(): pl.pallas_call(functools.partial(kernel, n_seg, n_tok, groups, per_group)...  28.6 us
    unnamed x1, local copies, waits for them, and re-layouts  2.3 us

profile of v3, /device:TPU:5, one launch (start us, length us, event | category | flops | bytes accessed | tf_op | source)
XLA Modules:
  0.0 30.9 jit_solution(15877311253468486605)
XLA Ops:
  0.0 28.6 %shard_map.64 = bf16[256,2048]{1,0:T(8,128)(2,1)} custom-call(bf16[256,2048]{1,0:T(8,128)(2,1)} %q_hbm.1, bf16[256,512]{1,0:T(8,128)(2,1)} %k_hbm.1, bf16[256,512]{1,0:T(8,128)(2,1)} %v_hbm.1, f32[1,2048]{1,0:T(1,128)} %bitcast.2, f32[1,2048]{1,0:T(1,128)} %bitcast.3, bf16[2048,2048]{1,0:T(8,128)(2,1)} %weight_hbm.1), custom_call_target="tpu_custom_call" | custom-call | tf_op jit(solution)/shard_map/pallas_call | solution.py:303
  28.6 2.3 %copy.8 = bf16[256,2048]{1,0:T(8,128)(2,1)} copy(bf16[256,2048]{1,0:T(8,128)(2,1)} %shard_map.64) | data formatting | bytes 2097152
